TPU v7x, 512 devices: a whole 4x4x16 slice. The times are simulated.
512 devices in a mesh: dp: 128 (over z, x, core), mp: 4 (over y).
Axes of the slice: x: 4, y: 4, z: 16, core: 2. Of those that a mesh axis runs over, the one named last changes fastest.
Arguments:
- queries: bfloat16 [114688, 2048], P('dp', 'mp'), may hold values from -20 to 20
- out_grad: bfloat16 [114688, 2048], P('dp', 'mp'), may hold values from -6 to 6
- store: bfloat16 [2048, 64, 512], P('dp', None, 'mp'), may hold values from -7 to 7
- key_weight: bfloat16 [512, 2048], P('dp', 'mp'), may hold values from -1 to 1
- value_weight: bfloat16 [512, 2048], P('dp', 'mp'), may hold values from -0.25 to 0.25
- owner: int32 [1792, 2], P('dp'), may hold values from 0 to 127, all different within a row; in each aligned block of 14 rows (0 to 13, 14 to 27, ...) no two rows name the same one
- row: int32 [1792, 2], P('dp'), may hold values from 0 to 15
- valid: int32 [1792, 2], P('dp'), may hold values from 16 to 64
Outputs:
- attended: bfloat16 [114688, 2048], P('dp', 'mp')
- key_grad: float32 [512, 2048], P('dp', 'mp')
- value_grad: float32 [512, 2048], P('dp', 'mp')
Inputs may be any that keep to these rules, and one draw needn't show every extreme that they name: Within the 14 query blocks of one index of dp (aligned blocks of rows) no owner is named more than 1 times, a bound that some block reaches; the 2 neighbours of one query block have different owners; every owner is named somewhere.
All inputs are finite; a program needn't handle non-finite values.
Results may differ from a plain program's by a relative error of at most 0.009.
The roundings to bfloat16 on the way count: a program that leaves them out, or rounds other values in their place, can miss the bound.
Values may be sent and summed in bfloat16 or wider, within the bound.
A program may use at most 64 MiB of HBM per device.

v0:
```python
import math

import jax
import jax.numpy as jnp
from jax import lax
from jax.sharding import PartitionSpec as P

HEAD_DIM = 128
ENC_WIDTH = 512
BLOCK_LEN = 64
NEIGH = 2
NB_LEN = 64


def shards(queries, out_grad, store, key_weight, value_weight, owner, row, valid):
    factor = 1.0 / math.sqrt(HEAD_DIM)
    peer_count = lax.axis_size("dp")
    block_count = queries.shape[0] // BLOCK_LEN
    request_count = block_count * NEIGH
    capacity = request_count // peer_count + 1
    head_width = key_weight.shape[1]
    head_count = head_width // HEAD_DIM
    flat_owner = owner.reshape(request_count)
    flat_row = row.reshape(request_count)
    position = lax.iota(jnp.int32, request_count)
    earlier_same = (flat_owner[:, None] == flat_owner[None, :]) & (
        position[None, :] < position[:, None]
    )
    slot_index = jnp.sum(earlier_same.astype(jnp.int32), axis=1)
    target = flat_owner * capacity + slot_index
    cell_ids = lax.iota(jnp.int32, peer_count * capacity)
    matches = cell_ids[:, None] == target[None, :]
    wanted = jnp.sum(jnp.where(matches, flat_row[None, :], 0), axis=1).reshape(peer_count, capacity)
    asked_rows = lax.all_to_all(wanted, "dp", split_axis=0, concat_axis=0, tiled=True).reshape(
        peer_count * capacity
    )
    picked = jnp.take(store, asked_rows, axis=0).reshape(
        peer_count, capacity, NB_LEN, store.shape[2]
    )
    returned = lax.all_to_all(picked, "dp", split_axis=0, concat_axis=0, tiled=True)
    own_slices = jnp.take(
        returned.reshape(peer_count * capacity, NB_LEN, store.shape[2]), target, axis=0
    )
    neighbours = lax.all_gather(own_slices, "mp", axis=2, tiled=True)
    flat_rows = neighbours.reshape(request_count * NB_LEN, ENC_WIDTH)
    key_full, value_full = (
        lax.all_gather(key_weight, "dp", axis=0, tiled=True),
        lax.all_gather(value_weight, "dp", axis=0, tiled=True),
    )
    key_sum = jnp.dot(flat_rows, key_full, preferred_element_type=jnp.float32)
    value_sum = jnp.dot(flat_rows, value_full, preferred_element_type=jnp.float32)
    key_heads = key_sum.astype(jnp.bfloat16).reshape(
        block_count, NEIGH * NB_LEN, head_count, HEAD_DIM
    )
    value_heads = value_sum.astype(jnp.bfloat16).reshape(
        block_count, NEIGH * NB_LEN, head_count, HEAD_DIM
    )
    query_heads = queries.reshape(block_count, BLOCK_LEN, head_count, HEAD_DIM)
    grad_heads = out_grad.reshape(block_count, BLOCK_LEN, head_count, HEAD_DIM)
    token_pos = lax.iota(jnp.int32, NB_LEN)
    allowed = (token_pos[None, None, :] < valid[:, :, None]).reshape(block_count, NEIGH * NB_LEN)
    scores = factor * jnp.einsum(
        "cihd,ckhd->chik", query_heads, key_heads, preferred_element_type=jnp.float32
    )
    scores = jnp.where(allowed[:, None, None, :], scores, -jnp.inf)
    highest = jnp.max(scores, axis=-1, keepdims=True)
    exponent = jnp.exp(scores - highest)
    probability = exponent / jnp.sum(exponent, axis=-1, keepdims=True)
    rounded = probability.astype(jnp.bfloat16)
    attended = jnp.einsum(
        "chik,ckhd->cihd", rounded, value_heads, preferred_element_type=jnp.float32
    ).astype(jnp.bfloat16)
    grad_prob = jnp.einsum(
        "cihd,ckhd->chik", grad_heads, value_heads, preferred_element_type=jnp.float32
    )
    grad_score = (
        probability * (grad_prob - jnp.sum(probability * grad_prob, axis=-1, keepdims=True))
    ).astype(jnp.bfloat16)
    key_cot = (
        factor
        * jnp.einsum("chik,cihd->ckhd", grad_score, query_heads, preferred_element_type=jnp.float32)
    ).astype(jnp.bfloat16)
    value_cot = jnp.einsum(
        "chik,cihd->ckhd", rounded, grad_heads, preferred_element_type=jnp.float32
    ).astype(jnp.bfloat16)
    both_cot = jnp.concatenate(
        [
            key_cot.reshape(flat_rows.shape[0], head_width),
            value_cot.reshape(flat_rows.shape[0], head_width),
        ],
        axis=1,
    )
    grads = lax.psum_scatter(
        lax.dot_general(
            flat_rows, both_cot, (((0,), (0,)), ((), ())), preferred_element_type=jnp.float32
        ),
        "dp",
        scatter_dimension=0,
        tiled=True,
    )
    return (
        attended.reshape(block_count * BLOCK_LEN, head_width),
        grads[:, :head_width],
        grads[:, head_width:],
    )


def solution(mesh):
    in_specs = (
        P("dp", "mp"),
        P("dp", "mp"),
        P("dp", None, "mp"),
        P("dp", "mp"),
        P("dp", "mp"),
        P("dp", None),
        P("dp", None),
        P("dp", None),
    )
    out_specs = (P("dp", "mp"), P("dp", "mp"), P("dp", "mp"))
    return jax.shard_map(shards, mesh=mesh, in_specs=in_specs, out_specs=out_specs, check_vma=False)
```

profile of v0, /device:TPU:1, one launch (start us, length us, event | category | flops | bytes accessed | tf_op | source)
XLA Modules:
  0.0 706.8 jit_solution(2045101588566621621)
XLA Ops:
  7.2 0.0 copy-start
  7.2 0.8 copy.66
  8.0 0.1 reshape.141
  8.1 0.2 convert_reduce_fusion
  8.3 0.8 copy.67
  9.0 0.1 broadcast_in_dim.56
  9.1 0.1 select_reduce_fusion
  9.2 0.1 copy.68
  9.3 35.1 %all_to_all.20 = s32[128,1,1]{2,1,0:T(1,128)S(1)} all-to-all(s32[128,1,1]{2,1,0:T(1,128)S(1)} %copy.68), channel_id=1, replica_groups=mesh['dp'=128,'mp'=4] {'dp'}, dimensions={0} | all-to-all | bytes 1024 | tf_op jit(solution)/shard_map/all_to_all | solution.py:34
  44.4 2.3 reduce
  46.8 0.0 copy-done
  46.8 1.0 gather_fusion
  47.8 1.6 bitcast_select_fusion
  49.4 5.7 all-to-all-start.1
  55.1 0.0 copy-start.7
  55.1 0.0 copy-start.5
  55.1 0.0 all-gather.4.cloned.1.call-start
  55.2 0.1 reshape.143
  55.3 96.7 %all-to-all-done.1 = bf16[128,1,64,128]{3,2,1,0:T(8,128)(2,1)S(1)} async-done(((bf16[128,1,64,128]{3,2,1,0:T(8,128)(2,1)}), bf16[128,1,64,128]{3,2,1,0:T(8,128)(2,1)S(1)}, u32[]{:S(2)}, u32[]{:S(2)}) %all-to-all-start.1) | async-done | bytes 2097184 | tf_op jit(solution)/shard_map/all_to_all | solution.py:40
  152.0 0.6 gather_fusion.1
  152.6 0.9 broadcast_select_fusion
  153.5 0.0 all-gather.4.cloned.1.call-update
  153.5 0.0 all-reduce.3.cloned.1.call-start
  153.6 0.1 lt.82
  153.7 0.0 copy-done.7
  153.7 0.1 copy.70
  153.8 0.1 lt.84
  153.9 0.1 lt.85
  153.9 0.0 copy-done.5
  153.9 84.2 %all-gather.1 = bf16[128,4,512]{2,1,0:T(4,128)(2,1)S(1)} all-gather(bf16[1,4,512]{2,1,0:T(4,128)(2,1)S(1)} %bitcast.68), channel_id=1, replica_groups=mesh['dp'=128,'mp'=4] {'dp'}, dimensions={0}, use_global_device_ids=true | all-gather | bytes 528384 | tf_op jit(solution)/shard_map/all_gather | solution.py:47
  238.1 0.9 reshape.171
  239.1 0.0 copy-done.6
  239.1 82.3 %all-gather = bf16[128,4,512]{2,1,0:T(4,128)(2,1)S(1)} all-gather(bf16[1,4,512]{2,1,0:T(4,128)(2,1)S(1)} %bitcast.69), channel_id=1, replica_groups=mesh['dp'=128,'mp'=4] {'dp'}, dimensions={0}, use_global_device_ids=true | all-gather | bytes 528384 | tf_op jit(solution)/shard_map/all_gather | solution.py:48
  321.3 0.1 reshape.169
  321.5 0.0 copy-done.2
  321.5 0.2 reshape.147
  321.7 2.6 reshape.149
  324.3 0.0 all-gather.4.cloned.1.call-done
  324.3 0.0 copy-done.4
  324.3 3.9 convolution_convert_fusion
  328.2 3.2 reshape.146
  331.4 3.9 convolution_convert_fusion.1
  335.3 4.2 reshape.145
  339.5 1.4 fusion.10
  340.9 3.0 fusion.43
  343.9 0.0 copy-start.9
  343.9 0.0 copy-done.3
  343.9 0.0 copy-start.1
  343.9 1.9 convert_bitcast_fusion
  345.8 0.2 copy-done.1
  346.1 1.7 fusion.5
  347.8 1.5 copy.80
  349.3 2.7 fusion.18
  352.0 1.5 copy.78
  353.5 0.7 copy_bitcast_fusion
  354.3 0.7 copy-done.8
  355.0 3.4 fusion.1
  358.4 0.0 all-reduce.3.cloned.1.call-update
  358.4 1.3 dynamic-slice
  360.3 2.2 fusion.22
  362.5 0.8 copy.74
  363.3 1.1 copy.109
  364.4 334.2 %all-reduce.3.cloned.1.call-done = f32[512,1024]{1,0:T(8,128)} async-done(((f32[512,1024]{1,0:T(8,128)}), f32[512,1024]{1,0:T(8,128)}) %all-reduce.3.cloned.1.call-update) | async-done | bytes 2097168
  698.6 1.4 fusion.42
  (14 shorter events, 0.1 us)
Async XLA Ops:
  7.2 39.7 %copy-start = (bf16[16,64,128]{2,1,0:T(8,128)(2,1)S(1)}, bf16[16,64,128]{2,1,0:T(8,128)(2,1)}, u32[]{:S(2)}) copy-start(bf16[16,64,128]{2,1,0:T(8,128)(2,1)} %param.10) | copy-start | bytes 786436
  49.4 102.6 %all-to-all-start.1 = ((bf16[128,1,64,128]{3,2,1,0:T(8,128)(2,1)}), bf16[128,1,64,128]{3,2,1,0:T(8,128)(2,1)S(1)}, u32[]{:S(2)}, u32[]{:S(2)}) async-start(bf16[128,1,64,128]{3,2,1,0:T(8,128)(2,1)} %bitcast_select_fusion), calls=%async_computation.1 | async-start | bytes 4194304 | tf_op jit(solution)/shard_map/all_to_all | solution.py:40
  55.1 98.6 %copy-start.7 = (s32[14,2]{0,1:T(2,128)S(1)}, s32[14,2]{0,1:T(2,128)}, u32[]{:S(2)}) copy-start(s32[14,2]{0,1:T(2,128)} %param.15) | copy-start | bytes 340
  55.1 98.8 %copy-start.5 = (bf16[4,512]{1,0:T(4,128)(2,1)S(1)}, bf16[4,512]{1,0:T(4,128)(2,1)}, u32[]{:S(2)}) copy-start(bf16[4,512]{1,0:T(4,128)(2,1)} %param.11) | copy-start | bytes 12292
  55.1 269.2 %all-gather.4.cloned.1.call-start = ((), (), s32[]{:S(2)}) async-start(), calls=%async_computation.2 | async-start | bytes 2293760 | tf_op jit(solution)/shard_map/all_gather | solution.py:44
  152.0 87.1 %copy-start.6 = (bf16[4,512]{1,0:T(4,128)(2,1)S(1)}, bf16[4,512]{1,0:T(4,128)(2,1)}, u32[]{:S(2)}) copy-start(bf16[4,512]{1,0:T(4,128)(2,1)} %param.12) | copy-start | bytes 12292
  153.5 168.0 %copy-start.2 = (bf16[896,512]{1,0:T(8,128)(2,1)S(1)}, bf16[896,512]{1,0:T(8,128)(2,1)}, u32[]{:S(2)}) copy-start(bf16[896,512]{1,0:T(8,128)(2,1)} %param.8) | copy-start | bytes 2752516
  153.5 545.0 %all-reduce.3.cloned.1.call-start = ((), (), s32[]{:S(2)}) async-start(), calls=%async_computation.3 | async-start | bytes 4194304
  321.5 2.9 copy-start.4
  340.9 3.0 copy-start.3
  343.9 5.4 copy-start.9
  343.9 2.2 copy-start.1
  353.5 1.5 copy-start.8
Sparse Core Ops, SparseCore 0:
  153.7 34.2 all-gather.3
  358.5 339.9 all-reduce.2
where the time goes:
time: 708 us; the launch traced here: 707 us
  waiting for transfers between devices  431 us (61%)
  blocking collectives  202 us (29%)
  local copies, waits for them, and re-layouts  24.5 us (3%)
  matrix products  21 us (3%)
  between operations  15 us (2%)
  other arithmetic  8.13 us (1%)
    unnamed x3, waiting for transfers between devices  334 us
    all_to_all x1, waiting for transfers between devices, shards(): lax.all_to_all(picked, 'dp', split_axis=0, concat_axis=0, tiled=True)  96.7 us
    all_gather x1, blocking collectives, shards(): lax.all_gather(key_weight, 'dp', axis=0, tiled=True)  84.2 us
    all_gather x1, blocking collectives, shards(): lax.all_gather(value_weight, 'dp', axis=0, tiled=True)  82.3 us
    all_to_all x1, blocking collectives, shards(): lax.all_to_all(wanted, 'dp', split_axis=0, concat_axis=0, tiled=True)  35.1 us
  transfers between devices with their start and end apart: 3, of which 2 were waited for; matrix products, arithmetic and copies ran while one was open for 1% of the time, Pallas kernels for 0%

commit v1 on v0

v1 whole, which is shorter than its diff:
```python
import functools
import math

import jax
import jax.numpy as jnp
from jax import lax
from jax.experimental import pallas as pl
from jax.experimental.pallas import tpu as pltpu
from jax.sharding import PartitionSpec as P

HEAD_DIM = 128
ENC_WIDTH = 512
BLOCK_LEN = 64
NEIGH = 2
NB_LEN = 64
BLOCKS = 14
SLOTS = BLOCKS * NEIGH
ROWS = SLOTS * NB_LEN
HEADS_DEV = 4
WIDTH = HEADS_DEV * HEAD_DIM
NZ, NX, NY, PLANE = 16, 4, 4, 8
CHUNKS = 7
PER = SLOTS // CHUNKS

MESH = pl.DeviceIdType.MESH
F32 = jnp.float32
BF16 = jnp.bfloat16
VM = pltpu.VMEM
VSPEC = pl.BlockSpec(memory_space=pltpu.VMEM)
SSPEC = pl.BlockSpec(memory_space=pltpu.SMEM)
VLIMIT = 56 * 2**20


def remote(src, dst, send, recv, device):
    return pltpu.make_async_remote_copy(
        src_ref=src,
        dst_ref=dst,
        send_sem=send,
        recv_sem=recv,
        device_id=device,
        device_id_type=MESH,
    )


def greet(devices):
    barrier = pltpu.get_barrier_semaphore()
    for device in devices:
        pl.semaphore_signal(barrier, inc=1, device_id=device, device_id_type=MESH)
    pl.semaphore_wait(barrier, len(devices))


def fetch_kernel(
    store, kw, vw, owner_v, row_v, owner_s, nb, wout, *scratch
):
    planes = scratch[:15]
    tab_v, tab_s, stage, got, wall = scratch[15:20]
    sems = scratch[20:]
    ring_s, ring_r, wring_s, wring_r, cell_s, cell_r, wc_s, wc_r = sems[:8]
    tab_ss, tab_rs, tab_ls, ys_s, ys_r, yf_s, yf_r = sems[8:]
    ups = [store] + [planes[2 * s - 2] for s in range(1, 8)] + [planes[14]]
    dns = [store] + [planes[2 * s - 1] for s in range(1, 8)] + [planes[14]]
    me = lax.axis_index("dp")
    y = lax.axis_index("mp")
    z, r = me // PLANE, me % PLANE
    zup = (((z + 1) % NZ) * PLANE + r, y)
    zdn = (((z + NZ - 1) % NZ) * PLANE + r, y)
    peer = [(z * PLANE + (r + t) % PLANE, y) for t in range(PLANE)]
    yup, ydn = (me, (y + 1) % NY), (me, (y + NY - 1) % NY)
    greet([zup, zdn] + peer[1:] + [yup, ydn])

    lane = lax.broadcasted_iota(jnp.int32, (BLOCKS, 128), 1)
    wanted = jnp.zeros((BLOCKS, 128), jnp.int32)
    for j in range(NEIGH):
        wanted = wanted + jnp.where(owner_v[:, j : j + 1] == lane, row_v[:, j : j + 1], 0)
    tab_v[r] = jnp.sum(wanted, axis=0, keepdims=True)
    both = jnp.concatenate([kw[...].astype(F32), vw[...].astype(F32)], axis=0)
    wall[r, 0] = jnp.concatenate([both[:, :256], both[:, 256:]], axis=0).astype(BF16)

    tab_copies = [
        remote(tab_v.at[r], tab_v.at[r], tab_ss.at[t], tab_rs.at[t], peer[t])
        for t in range(1, PLANE)
    ]
    for copy in tab_copies:
        copy.start()

    def ring(s, way, part):
        bufs = (ups, dns)[way]
        piece = pl.ds(part * 8, 8)
        return remote(
            bufs[s].at[piece],
            bufs[s + 1].at[piece],
            ring_s.at[way, s, part],
            ring_r.at[way, s, part],
            (zup, zdn)[way],
        )

    def place(s, way):
        return 0 if s == 0 else 15 if s == 8 else 2 * s - 1 + way

    def weight_ring(s, way):
        return remote(
            wall.at[r, place(s, way)],
            wall.at[r, place(s + 1, way)],
            wring_s.at[way, s],
            wring_r.at[way, s],
            (zup, zdn)[way],
        )

    waits = []
    for s in range(9):
        ways = (0,) if s == 7 else (0, 1)
        if s > 0:
            for way in (0,) if s == 8 else (0, 1):
                weight_ring(s - 1, way).wait_recv()
        if s < 8:
            for way in ways:
                copy = weight_ring(s, way)
                copy.start()
                waits.append(copy)
        for part in range(2):
            for way in range(2):
                if s > 0 and not (s == 8 and part != way):
                    ring(s - 1, way, part).wait_recv()
                if s < 8 and not (s == 7 and part != way):
                    copy = ring(s, way, part)
                    copy.start()
                    waits.append(copy)
        if s == 0:
            for copy in tab_copies:
                copy.wait()
            local = pltpu.make_async_copy(tab_v, tab_s, tab_ls)
            local.start()
            local.wait()
        first, count = place(s, 0), 1 if s in (0, 8) else 2
        for n in range(count):
            buf = (ups, dns)[n][s]
            far = (z + NZ - s) % NZ if n == 0 else (z + s) % NZ
            for t in range(PLANE):
                entry = buf[tab_s[(r + t) % PLANE, 0, far * PLANE + r]]
                if t == 0:
                    got[r, first + n] = entry
                else:
                    stage[t, first + n] = entry
        cut = pl.ds(first, count)
        for t in range(1, PLANE):
            for copy in (
                remote(
                    wall.at[r, cut], wall.at[r, cut], wc_s.at[t, s], wc_r.at[t, s], peer[t]
                ),
                remote(
                    stage.at[t, cut], got.at[r, cut], cell_s.at[t, s], cell_r.at[t, s], peer[t]
                ),
            ):
                copy.start()
                waits.append(copy)
    for s in range(9):
        cut = pl.ds(place(s, 0), 1 if s in (0, 8) else 2)
        for t in range(1, PLANE):
            remote(
                stage.at[t, cut], got.at[r, cut], cell_s.at[t, s], cell_r.at[t, s], peer[t]
            ).wait_recv()

    y_copies = []
    for g in range(CHUNKS):
        for i in range(g * PER, (g + 1) * PER):
            o = owner_s[i // NEIGH, i % NEIGH]
            zo = o // PLANE
            rel = (zo - z + NZ) % NZ
            where_k = jnp.where(rel < 8, 2 * rel, 31 - 2 * rel)
            nb[y, i] = got[o % PLANE, where_k]
        piece = pl.ds(g * PER, PER)
        for way in range(2):
            copy = remote(
                nb.at[y, piece], nb.at[y, piece], ys_s.at[way, g], ys_r.at[way, g], (yup, ydn)[way]
            )
            copy.start()
            y_copies.append(copy)

    for s in range(9):
        cut = pl.ds(place(s, 0), 1 if s in (0, 8) else 2)
        for t in range(1, PLANE):
            remote(
                wall.at[r, cut], wall.at[r, cut], wc_s.at[t, s], wc_r.at[t, s], peer[t]
            ).wait_recv()
    line = lax.broadcasted_iota(jnp.int32, (64, 128), 0)
    column = lax.broadcasted_iota(jnp.int32, (64, 128), 1)
    line = (line % 32) // 4 * 16 + line // 32 * 4 + line % 4
    for k in range(16):
        if k == 0:
            zo = z
        elif k == 15:
            zo = (z + 8) % NZ
        else:
            d = (k + 1) // 2
            zo = (z + NZ - d) % NZ if k % 2 else (z + d) % NZ
        tiles = wall[:, k].reshape(128, 256)
        at = pl.ds(pl.multiple_of(zo * 32, 32), 32)
        for half in range(2):
            pick = jnp.where(line + half * 8 == column, 1.0, 0.0).astype(BF16)
            sorted_rows = jnp.dot(pick, tiles, preferred_element_type=F32).astype(BF16)
            wout[at, half * 256 : half * 256 + 256] = sorted_rows[:32]
            wout[at, WIDTH + half * 256 : WIDTH + half * 256 + 256] = sorted_rows[32:]

    forwards = []
    for g in range(CHUNKS):
        piece = pl.ds(g * PER, PER)
        way = g % 2
        for w in range(2):
            y_copies[2 * g + w].wait_recv()
        origin = (y + NY - 1) % NY if way == 0 else (y + 1) % NY
        copy = remote(
            nb.at[origin, piece], nb.at[origin, piece], yf_s.at[g], yf_r.at[g], (yup, ydn)[way]
        )
        copy.start()
        forwards.append(copy)
    for copy in waits + y_copies:
        copy.wait_send()
    for copy in forwards:
        copy.wait()


def fetch(store, key_weight, value_weight, owner, row):
    dma = pltpu.SemaphoreType.DMA
    return pl.pallas_call(
        fetch_kernel,
        out_shape=(
            jax.ShapeDtypeStruct((NY, SLOTS, NB_LEN, 128), BF16),
            jax.ShapeDtypeStruct((ENC_WIDTH, 2 * WIDTH), BF16),
        ),
        in_specs=[VSPEC] * 5 + [SSPEC],
        out_specs=(VSPEC, VSPEC),
        scratch_shapes=[VM((16, NB_LEN, 128), BF16)] * 15
        + [
            VM((PLANE, 1, 128), jnp.int32),
            pltpu.SMEM((PLANE, 1, 128), jnp.int32),
            VM((PLANE, 16, NB_LEN, 128), BF16),
            VM((PLANE, 16, NB_LEN, 128), BF16),
            VM((PLANE, 16, 16, 256), BF16),
            dma((2, 8, 2)),
            dma((2, 8, 2)),
            dma((2, 8)),
            dma((2, 8)),
            dma((PLANE, 9)),
            dma((PLANE, 9)),
            dma((PLANE, 9)),
            dma((PLANE, 9)),
            dma((PLANE,)),
            dma((PLANE,)),
            dma,
            dma((2, CHUNKS)),
            dma((2, CHUNKS)),
            dma((CHUNKS,)),
            dma((CHUNKS,)),
        ],
        compiler_params=pltpu.CompilerParams(
            collective_id=0, has_side_effects=True, vmem_limit_bytes=VLIMIT
        ),
    )(store, key_weight, value_weight, owner, row, owner)


def dot_t(a, b):
    return lax.dot_general(a, b, (((1,), (1,)), ((), ())), preferred_element_type=F32)


def t_dot(a, b):
    return lax.dot_general(a, b, (((0,), (0,)), ((), ())), preferred_element_type=F32)


def attend_kernel(nb, weights, queries, grads, valid, attended, cot, rows_t):
    factor = 1.0 / math.sqrt(HEAD_DIM)
    key_pos = lax.broadcasted_iota(jnp.int32, (1, NEIGH * NB_LEN), 1)

    for g in range(CHUNKS):
        rows = jnp.concatenate(
            [nb[f, g * PER : (g + 1) * PER].reshape(PER * NB_LEN, 128) for f in range(NY)], axis=1
        )
        rows_t[:, g * 256 : (g + 1) * 256] = rows.T
        states = jnp.dot(rows, weights[...], preferred_element_type=F32).astype(BF16)
        for b in range(2):
            block = 2 * g + b
            first, second = valid[block, 0], valid[block, 1]
            allowed = (key_pos < first) | ((key_pos >= NB_LEN) & (key_pos < NB_LEN + second))
            at = pl.ds(block * BLOCK_LEN, BLOCK_LEN)
            to = pl.ds(block * 128, 128)
            for h in range(HEADS_DEV):
                lanes = slice(h * 128, h * 128 + 128)
                key = states[b * 128 : b * 128 + 128, h * 128 : h * 128 + 128]
                value = states[b * 128 : b * 128 + 128, WIDTH + h * 128 : WIDTH + h * 128 + 128]
                query, grad = queries[at, lanes], grads[at, lanes]
                scores = jnp.where(allowed, factor * dot_t(query, key), -jnp.inf)
                exponent = jnp.exp(scores - jnp.max(scores, axis=1, keepdims=True))
                prob = exponent / jnp.sum(exponent, axis=1, keepdims=True)
                rounded = prob.astype(BF16)
                attended[at, lanes] = jnp.dot(
                    rounded, value, preferred_element_type=F32
                ).astype(BF16)
                grad_prob = dot_t(grad, value)
                inner = jnp.sum(prob * grad_prob, axis=1, keepdims=True)
                grad_score = (prob * (grad_prob - inner)).astype(BF16)
                cot[to, lanes] = (factor * t_dot(grad_score, query)).astype(BF16)
                cot[to, WIDTH + h * 128 : WIDTH + h * 128 + 128] = t_dot(rounded, grad).astype(BF16)


def attend(nb, weights, queries, grads, valid):
    return pl.pallas_call(
        attend_kernel,
        out_shape=(
            jax.ShapeDtypeStruct((BLOCKS * BLOCK_LEN, WIDTH), BF16),
            jax.ShapeDtypeStruct((ROWS, 2 * WIDTH), BF16),
            jax.ShapeDtypeStruct((ENC_WIDTH, ROWS), BF16),
        ),
        in_specs=[VSPEC] * 4 + [SSPEC],
        out_specs=(VSPEC,) * 3,
        compiler_params=pltpu.CompilerParams(vmem_limit_bytes=VLIMIT),
    )(nb, weights, queries, grads, valid)


def reduce_kernel(rows_t, cot, key_out, value_out, *scratch):
    c_send, c_recv, total, x_send, x_recv, own, z_send, z_recv, fin, fin_in = scratch[:10]
    cs, cr, xs, xr, zs, zr, fs, fr = scratch[10:]
    me = lax.axis_index("dp")
    y = lax.axis_index("mp")
    z, x, c = me // PLANE, (me % PLANE) // 2, me % 2
    mate = (me + 1 - 2 * c, y)
    x_peer = [(z * PLANE + ((x + t) % NX) * 2 + c, y) for t in range(1, NX)]
    z_peer = [(((z + t) % NZ) * PLANE + x * 2 + c, y) for t in range(1, NZ)]
    greet([mate] + x_peer + z_peer)

    core_copies, x_copies, z_copies = [], [], []
    for h in range(2):
        theirs = pl.ds(pl.multiple_of((1 - c) * WIDTH + h * 256, 128), 256)
        mine = pl.ds(pl.multiple_of(c * WIDTH + h * 256, 128), 256)
        c_send[h] = jnp.dot(rows_t[...], cot[:, theirs], preferred_element_type=F32)
        copy = remote(c_send.at[h], c_recv.at[h], cs.at[h], cr.at[h], mate)
        copy.start()
        core_copies.append(copy)
        total[h] = jnp.dot(
            rows_t[...], cot[:, mine], preferred_element_type=F32
        ).reshape(NZ, NX, 8, 256)
    for h in range(2):
        core_copies[h].wait_recv()
        total[h] = total[h] + c_recv[h].reshape(NZ, NX, 8, 256)
        for t in range(1, NX):
            x_send[h, t - 1] = total[h, :, (x + t) % NX].reshape(128, 256).astype(BF16)
            copy = remote(
                x_send.at[h, t - 1], x_recv.at[h, t - 1], xs.at[h, t - 1], xr.at[h, t - 1], x_peer[t - 1]
            )
            copy.start()
            x_copies.append(copy)
    for h in range(2):
        line_sum = total[h, :, x]
        for t in range(1, NX):
            x_copies[h * 3 + t - 1].wait_recv()
            line_sum = line_sum + x_recv[h, t - 1].astype(F32).reshape(NZ, 8, 256)
        line_sum = jnp.concatenate([line_sum[:, :, :128], line_sum[:, :, 128:]], axis=1)
        own[h] = line_sum
        z_send[h] = line_sum.astype(BF16)
        for t in range(1, NZ):
            copy = remote(
                z_send.at[h, (z + t) % NZ],
                z_recv.at[h, t - 1],
                zs.at[h, t - 1],
                zr.at[h, t - 1],
                z_peer[t - 1],
            )
            copy.start()
            z_copies.append(copy)
    for h in range(2):
        done = own[h, z]
        for t in range(1, NZ):
            z_copies[h * 15 + t - 1].wait_recv()
            done = done + z_recv[h, t - 1].astype(F32)
        fin[:, h * 256 : h * 256 + 128] = done[:8]
        fin[:, h * 256 + 128 : h * 256 + 256] = done[8:]
    last = remote(fin, fin_in, fs, fr, mate)
    last.start()
    for copy in core_copies + x_copies + z_copies:
        copy.wait_send()
    last.wait()
    even = c == 0
    mine = jnp.where(even, fin[:4], fin[4:])
    theirs = jnp.where(even, fin_in[:4], fin_in[4:])
    key_out[...] = jnp.where(even, mine, theirs)
    value_out[...] = jnp.where(even, theirs, mine)


def reduce(rows_t, cot):
    dma = pltpu.SemaphoreType.DMA
    return pl.pallas_call(
        reduce_kernel,
        out_shape=(jax.ShapeDtypeStruct((4, WIDTH), F32),) * 2,
        in_specs=[VSPEC] * 2,
        out_specs=(VSPEC,) * 2,
        scratch_shapes=[
            VM((2, ENC_WIDTH, 256), F32),
            VM((2, ENC_WIDTH, 256), F32),
            VM((2, NZ, NX, 8, 256), F32),
            VM((2, NX - 1, 128, 256), BF16),
            VM((2, NX - 1, 128, 256), BF16),
            VM((2, NZ, 16, 128), F32),
            VM((2, NZ, 16, 128), BF16),
            VM((2, NZ - 1, 16, 128), BF16),
            VM((8, WIDTH), F32),
            VM((8, WIDTH), F32),
            dma((2,)),
            dma((2,)),
            dma((2, NX - 1)),
            dma((2, NX - 1)),
            dma((2, NZ - 1)),
            dma((2, NZ - 1)),
            dma,
            dma,
        ],
        compiler_params=pltpu.CompilerParams(
            collective_id=1, has_side_effects=True, vmem_limit_bytes=VLIMIT
        ),
    )(rows_t, cot)


def shards(queries, out_grad, store, key_weight, value_weight, owner, row, valid):
    nb, weights = fetch(store, key_weight, value_weight, owner, row)
    attended, cot, rows_t = attend(nb, weights, queries, out_grad, valid)
    key_grad, value_grad = reduce(rows_t, cot)
    return attended, key_grad, value_grad


def solution(mesh):
    in_specs = (
        P("dp", "mp"),
        P("dp", "mp"),
        P("dp", None, "mp"),
        P("dp", "mp"),
        P("dp", "mp"),
        P("dp", None),
        P("dp", None),
        P("dp", None),
    )
    out_specs = (P("dp", "mp"), P("dp", "mp"), P("dp", "mp"))
    return jax.shard_map(shards, mesh=mesh, in_specs=in_specs, out_specs=out_specs, check_vma=False)
```

time: 708 us -> 157 us (0.22)
  waiting for transfers between devices: 431 us -> 0 us
  blocking collectives: 202 us -> 0 us
  Pallas kernels: 0 us -> 150 us
  matrix products: 21 us -> 0 us
  local copies, waits for them, and re-layouts: 24.5 us -> 6.66 us
  between operations: 15 us -> 0.65 us
  other arithmetic: 8.13 us -> 0 us
    unnamed x3 -> x0, waiting for transfers between devices: 334 us -> none
    all_gather x2 -> x0, blocking collectives: 166 us -> none  [the longest x1 84.2 us: shards(): lax.all_gather(key_weight, 'dp', axis=0, tiled=True)]
    pallas_call x0 -> x3, Pallas kernels: none -> 150 us  [the longest x1 89.4 us: fetch(): pl.pallas_call(fetch_kernel, out_shape=(jax.ShapeDtypeStruct((NY, SLOTS,...]
    all_to_all x1 -> x0, waiting for transfers between devices: 96.7 us -> none  [shards(): lax.all_to_all(picked, 'dp', split_axis=0, concat_axis=0, tiled=True)]
    all_to_all x1 -> x0, blocking collectives: 35.1 us -> none  [shards(): lax.all_to_all(wanted, 'dp', split_axis=0, concat_axis=0, tiled=True)]
    dot_general x8 -> x0, matrix products: 21 us -> none  [the longest x1 3.87 us: shards(): jnp.dot(flat_rows, value_full, preferred_element_type=jnp.float32)]
    reshape x7 -> x0, local copies, waits for them, and re-layouts: 11.2 us -> none  [the longest x1 4.23 us: shards(): value_sum.astype(jnp.bfloat16)]
  transfers between devices with their start and end apart: 3 -> 0, of which waited for: 2 -> 0; matrix products, arithmetic and copies ran while one was open for 1% -> 0% of each run, Pallas kernels for 0% -> 0%
where the time goes in v1:
time: 157 us
  Pallas kernels  150 us (96%)
  local copies, waits for them, and re-layouts  6.66 us (4%)
    pallas_call x1, Pallas kernels, fetch(): pl.pallas_call(fetch_kernel, out_shape=(jax.ShapeDtypeStruct((NY, SLOTS,...  89.4 us
    pallas_call x1, Pallas kernels, reduce(): pl.pallas_call(reduce_kernel, out_shape=(jax.ShapeDtypeStruct((4, WIDTH),...  31.6 us
    pallas_call x1, Pallas kernels, attend(): pl.pallas_call(attend_kernel, out_shape=(jax.ShapeDtypeStruct((BLOCKS * B...  28.9 us
    unnamed x5, local copies, waits for them, and re-layouts  6.66 us

profile of v1, /device:TPU:1, one launch (start us, length us, event | category | flops | bytes accessed | tf_op | source)
XLA Modules:
  0.0 157.2 jit_solution(14014147410870512620)
XLA Ops:
  0.6 1.4 copy.11.owner_v.owner_s
  2.0 1.4 copy.12.row_v
  3.3 1.4 copy.14.valid
  4.7 89.4 %shard_map.103 = (bf16[4,28,64,128]{3,2,1,0:T(8,128)(2,1)}, bf16[512,1024]{1,0:T(8,128)(2,1)}) custom-call(bf16[16,64,128]{2,1,0:T(8,128)(2,1)} %store.1, bf16[4,512]{1,0:T(4,128)(2,1)} %kw.1, bf16[4,512]{1,0:T(4,128)(2,1)} %vw.1, s32[14,2]{1,0:T(8,128)} %copy.11.owner_v.owner_s, s32[14,2]{1,0:T(8,128)} %copy.12.row_v, s32[14,2]{1,0:T(8,128)} %copy.11.owner_v.owner_s), custom_call_target="tpu_custom_call" | custom-call | tf_op jit(solution)/shard_map/pallas_call | solution.py:224
  94.1 28.9 %shard_map.104 = (bf16[896,512]{1,0:T(8,128)(2,1)}, bf16[1792,1024]{1,0:T(8,128)(2,1)}, bf16[512,1792]{1,0:T(8,128)(2,1)}) custom-call(bf16[4,28,64,128]{3,2,1,0:T(8,128)(2,1)} %get-tuple-element.10.nb, bf16[512,1024]{1,0:T(8,128)(2,1)} %get-tuple-element.11.weights, bf16[896,512]{1,0:T(8,128)(2,1)} %queries.1, bf16[896,512]{1,0:T(8,128)(2,1)} %grads.1, ...), custom_call_target="tpu_custom_call" | custom-call | tf_op jit(solution)/shard_map/pallas_call | solution.py:305
  123.0 31.6 %shard_map.105 = (f32[4,512]{1,0:T(4,128)}, f32[4,512]{1,0:T(4,128)}) custom-call(bf16[512,1792]{1,0:T(8,128)(2,1)} %get-tuple-element.13.rows_t, bf16[1792,1024]{1,0:T(8,128)(2,1)} %get-tuple-element.14.cot), custom_call_target="tpu_custom_call" | custom-call | tf_op jit(solution)/shard_map/pallas_call | solution.py:389
  154.6 1.3 copy.17
  155.9 1.3 copy.18

commit v2 on v0

v2 whole, which is shorter than its diff:
```python
import functools
import math

import jax
import jax.numpy as jnp
from jax import lax
from jax.experimental import pallas as pl
from jax.experimental.pallas import tpu as pltpu
from jax.sharding import PartitionSpec as P

HEAD_DIM = 128
ENC_WIDTH = 512
BLOCK_LEN = 64
NEIGH = 2
NB_LEN = 64
BLOCKS = 14
SLOTS = BLOCKS * NEIGH
ROWS = SLOTS * NB_LEN
HEADS_DEV = 4
WIDTH = HEADS_DEV * HEAD_DIM
NZ, NX, NY, PLANE = 16, 4, 4, 8
CHUNKS = 7
PER = SLOTS // CHUNKS

MESH = pl.DeviceIdType.MESH
F32 = jnp.float32
BF16 = jnp.bfloat16
VM = pltpu.VMEM
VSPEC = pl.BlockSpec(memory_space=pltpu.VMEM)
SSPEC = pl.BlockSpec(memory_space=pltpu.SMEM)
VLIMIT = 56 * 2**20


def remote(src, dst, send, recv, device):
    return pltpu.make_async_remote_copy(
        src_ref=src,
        dst_ref=dst,
        send_sem=send,
        recv_sem=recv,
        device_id=device,
        device_id_type=MESH,
    )


def greet(devices):
    barrier = pltpu.get_barrier_semaphore()
    for device in devices:
        pl.semaphore_signal(barrier, inc=1, device_id=device, device_id_type=MESH)
    pl.semaphore_wait(barrier, len(devices))


def dot(a, b):
    return jnp.dot(a, b, preferred_element_type=F32)


def dot_t(a, b):
    return lax.dot_general(a, b, (((1,), (1,)), ((), ())), preferred_element_type=F32)


def attend_chunk(g, nb, weights, queries, grads, valid, attended, cot, rows_t):
    factor = 1.0 / math.sqrt(HEAD_DIM)
    rows = jnp.concatenate(
        [nb[f, g * PER : (g + 1) * PER].reshape(PER * NB_LEN, 128) for f in range(NY)], axis=1
    )
    states = dot(rows, weights[...]).astype(BF16)
    rows_t[:, g * 256 : (g + 1) * 256] = rows.T
    key_pos = lax.broadcasted_iota(jnp.int32, (NEIGH * NB_LEN, 2 * BLOCK_LEN), 0)
    zero = jnp.zeros((BLOCK_LEN, HEAD_DIM), BF16)

    def diagonal(ref, at, lane):
        return jnp.concatenate(
            [
                jnp.concatenate([ref[at, lane : lane + 128], zero], axis=1),
                jnp.concatenate([zero, ref[at, lane + 128 : lane + 256]], axis=1),
            ],
            axis=0,
        )

    for b in range(2):
        block = 2 * g + b
        first, second = valid[0, block], valid[1, block]
        allowed = (key_pos < first) | ((key_pos >= NB_LEN) & (key_pos < NB_LEN + second))
        at = slice(block * BLOCK_LEN, (block + 1) * BLOCK_LEN)
        to = slice(block * 128, block * 128 + 128)
        for lane in range(0, WIDTH, 256):
            key = states[b * 128 : b * 128 + 128, lane : lane + 256]
            value = states[b * 128 : b * 128 + 128, WIDTH + lane : WIDTH + lane + 256]
            query, grad = diagonal(queries, at, lane), diagonal(grads, at, lane)
            scores = jnp.where(allowed, factor * dot_t(key, query), -jnp.inf)
            exponent = jnp.exp(scores - jnp.max(scores, axis=0, keepdims=True))
            prob = exponent * (1.0 / jnp.sum(exponent, axis=0, keepdims=True))
            rounded = prob.astype(BF16)
            out = dot(rounded.T, value).astype(BF16)
            attended[at, lane : lane + 128] = out[:BLOCK_LEN, :128]
            attended[at, lane + 128 : lane + 256] = out[BLOCK_LEN:, 128:]
            grad_prob = dot_t(value, grad)
            inner = jnp.sum(prob * grad_prob, axis=0, keepdims=True)
            grad_score = (prob * (grad_prob - inner)).astype(BF16)
            cot[to, lane : lane + 256] = (factor * dot(grad_score, query)).astype(BF16)
            cot[to, WIDTH + lane : WIDTH + lane + 256] = dot(rounded, grad).astype(BF16)


def step_kernel(names, *refs):
    (store, kw, vw, owner_s, row_s, valid_s, queries_h, grads_h, attended_h, sums_out) = refs[:10]
    planes, named = refs[10:25], dict(zip(names, refs[25:]))
    S = lambda name: named[name]
    tab_v, tab_s, stage, got, wall = map(S, ("tab_v", "tab_s", "stage", "got", "wall"))
    nb, weights, queries, grads, attended = map(S, ("nb", "weights", "queries", "grads", "attended"))
    ups = [store] + [planes[2 * s - 2] for s in range(1, 8)] + [planes[14]]
    dns = [store] + [planes[2 * s - 1] for s in range(1, 8)] + [planes[14]]
    me = lax.axis_index("dp")
    y = lax.axis_index("mp")
    z, r = me // PLANE, me % PLANE
    x, c = r // 2, r % 2
    zup = (((z + 1) % NZ) * PLANE + r, y)
    zdn = (((z + NZ - 1) % NZ) * PLANE + r, y)
    peer = [(z * PLANE + (r + t) % PLANE, y) for t in range(PLANE)]
    yup, ydn = (me, (y + 1) % NY), (me, (y + NY - 1) % NY)
    mate = (me + 1 - 2 * c, y)
    x_peer = [(z * PLANE + ((x + t) % NX) * 2 + c, y) for t in range(1, NX)]
    z_peer = [(((z + t) % NZ) * PLANE + r, y) for t in range(1, NZ)]

    local_sem = S("local_sem")
    loads = [
        pltpu.make_async_copy(queries_h, queries, local_sem.at[0]),
        pltpu.make_async_copy(grads_h, grads, local_sem.at[1]),
    ]
    for copy in loads:
        copy.start()
    greet(peer[1:] + z_peer + [yup, ydn])

    lane = lax.broadcasted_iota(jnp.int32, (1, 128), 1)
    wanted = jnp.zeros((1, 128), jnp.int32)
    for j in range(NEIGH):
        for b in range(BLOCKS):
            wanted = wanted + jnp.where(lane == owner_s[j, b], row_s[j, b], 0)
    tab_v[r] = wanted
    both = jnp.concatenate([kw[...].astype(F32), vw[...].astype(F32)], axis=0)
    wall[r, 0] = jnp.concatenate([both[:, :256], both[:, 256:]], axis=0).astype(BF16)

    tab_copies = [
        remote(tab_v.at[r], tab_v.at[r], S("tab_ss").at[t], S("tab_rs").at[t], peer[t])
        for t in range(1, PLANE)
    ]
    for copy in tab_copies:
        copy.start()

    def ring(s, way, part):
        bufs = (ups, dns)[way]
        piece = pl.ds(part * 8, 8)
        return remote(
            bufs[s].at[piece],
            bufs[s + 1].at[piece],
            S("ring_s").at[way, s, part],
            S("ring_r").at[way, s, part],
            (zup, zdn)[way],
        )

    def place(s, way):
        return 0 if s == 0 else 15 if s == 8 else 2 * s - 1 + way

    def cut_of(s):
        return pl.ds(place(s, 0), 1 if s in (0, 8) else 2)

    def weight_ring(s, way):
        return remote(
            wall.at[r, place(s, way)],
            wall.at[r, place(s + 1, way)],
            S("wring_s").at[way, s],
            S("wring_r").at[way, s],
            (zup, zdn)[way],
        )

    def weight_plane(s, t):
        rows = wall.at[r, cut_of(s)]
        return remote(rows, rows, S("wc_s").at[t, s], S("wc_r").at[t, s], peer[t])

    def cell_plane(s, t):
        return remote(
            stage.at[t, cut_of(s)],
            got.at[r, cut_of(s)],
            S("cell_s").at[t, s],
            S("cell_r").at[t, s],
            peer[t],
        )

    line = lax.broadcasted_iota(jnp.int32, (64, 128), 0)
    column = lax.broadcasted_iota(jnp.int32, (64, 128), 1)
    line = (line % 32) // 4 * 16 + line // 32 * 4 + line % 4
    picks = [jnp.where(line + half * 8 == column, 1.0, 0.0).astype(BF16) for half in range(2)]

    def place_weights(s):
        for t in range(1, PLANE):
            weight_plane(s, t).wait_recv()
        for way in range(1 if s in (0, 8) else 2):
            far = (z + NZ - s) % NZ if way == 0 else (z + s) % NZ
            tiles = wall[:, place(s, way)].reshape(128, 256)
            at = pl.ds(pl.multiple_of(far * 32, 32), 32)
            for half in range(2):
                ordered = dot(picks[half], tiles).astype(BF16)
                weights[at, half * 256 : half * 256 + 256] = ordered[:32]
                weights[at, WIDTH + half * 256 : WIDTH + half * 256 + 256] = ordered[32:]

    sent = []
    for s in range(9):
        if s > 0:
            for way in (0,) if s == 8 else (0, 1):
                weight_ring(s - 1, way).wait_recv()
        if s < 8:
            for way in (0,) if s == 7 else (0, 1):
                copy = weight_ring(s, way)
                copy.start()
                sent.append(copy)
        for part in range(2):
            for way in range(2):
                if s > 0 and not (s == 8 and part != way):
                    ring(s - 1, way, part).wait_recv()
                if s < 8 and not (s == 7 and part != way):
                    copy = ring(s, way, part)
                    copy.start()
                    sent.append(copy)
        if s == 0:
            for copy in tab_copies:
                copy.wait()
            local = pltpu.make_async_copy(tab_v, tab_s, local_sem.at[2])
            local.start()
            local.wait()
        for way in range(1 if s in (0, 8) else 2):
            buf = (ups, dns)[way][s]
            far = (z + NZ - s) % NZ if way == 0 else (z + s) % NZ
            for t in range(PLANE):
                entry = buf[tab_s[(r + t) % PLANE, 0, far * PLANE + r]]
                if t == 0:
                    got[r, place(s, way)] = entry
                else:
                    stage[t, place(s, way)] = entry
        for t in range(1, PLANE):
            for copy in (weight_plane(s, t), cell_plane(s, t)):
                copy.start()
                sent.append(copy)
        if s >= 2:
            place_weights(s - 2)
    place_weights(7)
    for s in range(9):
        for t in range(1, PLANE):
            cell_plane(s, t).wait_recv()

    def own_y(g, way):
        part = nb.at[y, pl.ds(g * PER, PER)]
        return remote(part, part, S("ys_s").at[way, g], S("ys_r").at[way, g], (yup, ydn)[way])

    def forward_y(g):
        origin = (y + NY - 1) % NY if g % 2 == 0 else (y + 1) % NY
        part = nb.at[origin, pl.ds(g * PER, PER)]
        return remote(part, part, S("yf_s").at[g], S("yf_r").at[g], (yup, ydn)[g % 2])

    def send_own(g):
        for i in range(g * PER, (g + 1) * PER):
            o = owner_s[i % NEIGH, i // NEIGH]
            rel = (o // PLANE - z + NZ) % NZ
            nb[y, i] = got[o % PLANE, jnp.where(rel < 8, 2 * rel, 31 - 2 * rel)]
        for way in range(2):
            copy = own_y(g, way)
            copy.start()
            sent.append(copy)

    ahead = 3
    for g in range(ahead):
        send_own(g)
    place_weights(8)
    for copy in loads:
        copy.wait()
    stores = []

    def attend(g):
        forward_y(g).wait_recv()
        attend_chunk(
            g, nb, weights, queries, grads, valid_s, attended, S("cot"), S("rows_t")
        )
        piece = pl.ds(g * 128, 128)
        copy = pltpu.make_async_copy(
            attended.at[piece], attended_h.at[piece], S("out_sem").at[g]
        )
        copy.start()
        stores.append(copy)

    for g in range(CHUNKS):
        for way in range(2):
            own_y(g, way).wait_recv()
        copy = forward_y(g)
        copy.start()
        sent.append(copy)
        if g + ahead < CHUNKS:
            send_own(g + ahead)
        if g > 0:
            attend(g - 1)
    attend(CHUNKS - 1)

    rows_t, cot, total = S("rows_t"), S("cot"), S("total")
    c_send, c_recv, x_send, x_recv = map(S, ("c_send", "c_recv", "x_send", "x_recv"))
    own, z_send, z_recv = map(S, ("own", "z_send", "z_recv"))
    core_copies, x_copies, z_copies = [], [], []
    for h in range(2):
        theirs = pl.ds(pl.multiple_of((1 - c) * WIDTH + h * 256, 128), 256)
        c_send[h] = dot(rows_t[...], cot[:, theirs]).astype(BF16)
        copy = remote(c_send.at[h], c_recv.at[h], S("cs").at[h], S("cr").at[h], mate)
        copy.start()
        core_copies.append(copy)
    for h in range(2):
        mine = pl.ds(pl.multiple_of(c * WIDTH + h * 256, 128), 256)
        part = dot(rows_t[...], cot[:, mine])
        core_copies[h].wait_recv()
        total[h] = (part + c_recv[h].astype(F32)).reshape(NZ, NX, 8, 256)
        for t in range(1, NX):
            x_send[h, t - 1] = total[h, :, (x + t) % NX].reshape(128, 256).astype(BF16)
            copy = remote(
                x_send.at[h, t - 1],
                x_recv.at[h, t - 1],
                S("xs").at[h, t - 1],
                S("xr").at[h, t - 1],
                x_peer[t - 1],
            )
            copy.start()
            x_copies.append(copy)
    for h in range(2):
        line_sum = total[h, :, x]
        for t in range(1, NX):
            x_copies[h * 3 + t - 1].wait_recv()
            line_sum = line_sum + x_recv[h, t - 1].astype(F32).reshape(NZ, 8, 256)
        line_sum = jnp.concatenate([line_sum[:, :, :128], line_sum[:, :, 128:]], axis=1)
        own[h] = line_sum
        z_send[h] = line_sum.astype(BF16)
        for t in range(1, NZ):
            copy = remote(
                z_send.at[h, (z + t) % NZ],
                z_recv.at[h, t - 1],
                S("zs").at[h, t - 1],
                S("zr").at[h, t - 1],
                z_peer[t - 1],
            )
            copy.start()
            z_copies.append(copy)
    fin, fin_in = S("fin"), S("fin_in")
    for h in range(2):
        done = own[h, z]
        for t in range(1, NZ):
            z_copies[h * 15 + t - 1].wait_recv()
            done = done + z_recv[h, t - 1].astype(F32)
        fin[:, h * 256 : h * 256 + 128] = done[:8]
        fin[:, h * 256 + 128 : h * 256 + 256] = done[8:]
    last = remote(fin, fin_in, S("fs"), S("fr"), mate)
    last.start()
    for copy in sent + core_copies + x_copies + z_copies:
        copy.wait_send()
    for copy in stores:
        copy.wait()
    last.wait()
    even = c == 0
    sums_out[0] = jnp.where(even, fin[...], fin_in[...])
    sums_out[1] = jnp.where(even, fin_in[...], fin[...])


def step(queries, out_grad, store, key_weight, value_weight, owner, row, valid):
    dma = pltpu.SemaphoreType.DMA
    scratch = {
        "tab_v": VM((PLANE, 1, 128), jnp.int32),
        "tab_s": pltpu.SMEM((PLANE, 1, 128), jnp.int32),
        "stage": VM((PLANE, 16, NB_LEN, 128), BF16),
        "got": VM((PLANE, 16, NB_LEN, 128), BF16),
        "wall": VM((PLANE, 16, 16, 256), BF16),
        "nb": VM((NY, SLOTS, NB_LEN, 128), BF16),
        "weights": VM((ENC_WIDTH, 2 * WIDTH), BF16),
        "queries": VM((BLOCKS * BLOCK_LEN, WIDTH), BF16),
        "grads": VM((BLOCKS * BLOCK_LEN, WIDTH), BF16),
        "attended": VM((BLOCKS * BLOCK_LEN, WIDTH), BF16),
        "cot": VM((ROWS, 2 * WIDTH), BF16),
        "rows_t": VM((ENC_WIDTH, ROWS), BF16),
        "c_send": VM((2, ENC_WIDTH, 256), BF16),
        "c_recv": VM((2, ENC_WIDTH, 256), BF16),
        "total": VM((2, NZ, NX, 8, 256), F32),
        "x_send": VM((2, NX - 1, 128, 256), BF16),
        "x_recv": VM((2, NX - 1, 128, 256), BF16),
        "own": VM((2, NZ, 16, 128), F32),
        "z_send": VM((2, NZ, 16, 128), BF16),
        "z_recv": VM((2, NZ - 1, 16, 128), BF16),
        "fin": VM((8, WIDTH), F32),
        "fin_in": VM((8, WIDTH), F32),
        "local_sem": dma((3,)),
        "out_sem": dma((CHUNKS,)),
        "fs": dma,
        "fr": dma,
    }
    for send, recv, shape in (
        ("ring_s", "ring_r", (2, 8, 2)),
        ("wring_s", "wring_r", (2, 8)),
        ("cell_s", "cell_r", (PLANE, 9)),
        ("wc_s", "wc_r", (PLANE, 9)),
        ("tab_ss", "tab_rs", (PLANE,)),
        ("ys_s", "ys_r", (2, CHUNKS)),
        ("yf_s", "yf_r", (CHUNKS,)),
        ("cs", "cr", (2,)),
        ("xs", "xr", (2, NX - 1)),
        ("zs", "zr", (2, NZ - 1)),
    ):
        scratch[send] = dma(shape)
        scratch[recv] = dma(shape)
    anywhere = pl.BlockSpec(memory_space=pl.ANY)
    return pl.pallas_call(
        functools.partial(step_kernel, tuple(scratch)),
        out_shape=(
            jax.ShapeDtypeStruct((BLOCKS * BLOCK_LEN, WIDTH), BF16),
            jax.ShapeDtypeStruct((2, 8, WIDTH), F32),
        ),
        in_specs=[VSPEC] * 3 + [SSPEC] * 3 + [anywhere] * 2,
        out_specs=(anywhere, VSPEC),
        scratch_shapes=[VM((16, NB_LEN, 128), BF16)] * 15 + list(scratch.values()),
        compiler_params=pltpu.CompilerParams(
            collective_id=0, has_side_effects=True, vmem_limit_bytes=VLIMIT
        ),
    )(store, key_weight, value_weight, owner.T, row.T, valid.T, queries, out_grad)


def finish_kernel(attended_in, sums, attended, key_out, value_out, held, sem_in, sem_out):
    count = sem_in.shape[0]
    size = held.shape[0] // count
    pieces = [pl.ds(i * size, size) for i in range(count)]
    inward = [
        pltpu.make_async_copy(attended_in.at[piece], held.at[piece], sem_in.at[i])
        for i, piece in enumerate(pieces)
    ]
    outward = [
        pltpu.make_async_copy(held.at[piece], attended.at[piece], sem_out.at[i])
        for i, piece in enumerate(pieces)
    ]
    for copy in inward:
        copy.start()
    low = lax.axis_index("dp") % 2 == 0
    key_out[...] = jnp.where(low, sums[0, :4], sums[0, 4:])
    value_out[...] = jnp.where(low, sums[1, :4], sums[1, 4:])
    for i in range(count):
        inward[i].wait()
        outward[i].start()
    for copy in outward:
        copy.wait()


def finish(attended, sums):
    anywhere = pl.BlockSpec(memory_space=pl.ANY)
    dma = pltpu.SemaphoreType.DMA
    return pl.pallas_call(
        finish_kernel,
        out_shape=(
            jax.ShapeDtypeStruct(attended.shape, BF16),
            jax.ShapeDtypeStruct((4, WIDTH), F32),
            jax.ShapeDtypeStruct((4, WIDTH), F32),
        ),
        in_specs=[anywhere, VSPEC],
        out_specs=(anywhere, VSPEC, VSPEC),
        scratch_shapes=[VM(attended.shape, BF16), dma((CHUNKS,)), dma((CHUNKS,))],
        compiler_params=pltpu.CompilerParams(vmem_limit_bytes=VLIMIT),
    )(attended, sums)


def shards(queries, out_grad, store, key_weight, value_weight, owner, row, valid):
    attended, sums = step(
        queries, out_grad, store, key_weight, value_weight, owner, row, valid
    )
    return finish(attended, sums)


def solution(mesh):
    in_specs = (
        P("dp", "mp"),
        P("dp", "mp"),
        P("dp", None, "mp"),
        P("dp", "mp"),
        P("dp", "mp"),
        P("dp", None),
        P("dp", None),
        P("dp", None),
    )
    out_specs = (P("dp", "mp"), P("dp", "mp"), P("dp", "mp"))
    return jax.shard_map(shards, mesh=mesh, in_specs=in_specs, out_specs=out_specs, check_vma=False)
```

time: 708 us -> 126 us (0.18)
  waiting for transfers between devices: 431 us -> 0 us
  blocking collectives: 202 us -> 0 us
  Pallas kernels: 0 us -> 125 us
  local copies, waits for them, and re-layouts: 24.5 us -> 0 us
  matrix products: 21 us -> 0 us
  between operations: 15 us -> 0.8 us
  other arithmetic: 8.13 us -> 0 us
    unnamed x3 -> x0, waiting for transfers between devices: 334 us -> none
    all_gather x2 -> x0, blocking collectives: 166 us -> none  [the longest x1 84.2 us: shards(): lax.all_gather(key_weight, 'dp', axis=0, tiled=True)]
    pallas_call x0 -> x2, Pallas kernels: none -> 125 us  [the longest x1 122 us: step(): pl.pallas_call(functools.partial(step_kernel, tuple(scratch)), out_shape=...]
    all_to_all x1 -> x0, waiting for transfers between devices: 96.7 us -> none  [shards(): lax.all_to_all(picked, 'dp', split_axis=0, concat_axis=0, tiled=True)]
    all_to_all x1 -> x0, blocking collectives: 35.1 us -> none  [shards(): lax.all_to_all(wanted, 'dp', split_axis=0, concat_axis=0, tiled=True)]
    dot_general x8 -> x0, matrix products: 21 us -> none  [the longest x1 3.87 us: shards(): jnp.dot(flat_rows, value_full, preferred_element_type=jnp.float32)]
    reshape x7 -> x0, local copies, waits for them, and re-layouts: 11.2 us -> none  [the longest x1 4.23 us: shards(): value_sum.astype(jnp.bfloat16)]
  transfers between devices with their start and end apart: 3 -> 0, of which waited for: 2 -> 0; matrix products, arithmetic and copies ran while one was open for 1% -> 0% of each run, Pallas kernels for 0% -> 0%
where the time goes in v2:
time: 126 us
  Pallas kernels  125 us (99%)
    pallas_call x1, Pallas kernels, step(): pl.pallas_call(functools.partial(step_kernel, tuple(scratch)), out_shape=...  122 us
    pallas_call x1, Pallas kernels, finish(): pl.pallas_call(finish_kernel, out_shape=(jax.ShapeDtypeStruct(attended.sh...  3.39 us

profile of v2, /device:TPU:1, one launch (start us, length us, event | category | flops | bytes accessed | tf_op | source)
XLA Modules:
  0.0 125.8 jit_solution(7838041234055499723)
XLA Ops:
  0.6 121.6 %shard_map.103 = (bf16[896,512]{1,0:T(8,128)(2,1)}, f32[2,8,512]{2,1,0:T(8,128)}) custom-call(bf16[16,64,128]{2,1,0:T(8,128)(2,1)} %refs_0_.1, bf16[4,512]{1,0:T(4,128)(2,1)} %refs_1_.1, bf16[4,512]{1,0:T(4,128)(2,1)} %refs_2_.1, s32[2,14]{1,0:T(2,128)} %bitcast.3, s32[2,14]{1,0:T(2,128)} %bitcast.4, s32[2,14]{1,0:T(2,128)} %bitcast.5, ...), custom_call_target="tpu_custom_call" | custom-call | tf_op jit(solution)/shard_map/pallas_call | solution.py:408
  122.3 3.4 %shard_map.104 = (bf16[896,512]{1,0:T(8,128)(2,1)}, f32[4,512]{1,0:T(4,128)}, f32[4,512]{1,0:T(4,128)}) custom-call(bf16[896,512]{1,0:T(8,128)(2,1)} %get-tuple-element.5.attended_in, f32[2,8,512]{2,1,0:T(8,128)} %get-tuple-element.6.sums), custom_call_target="tpu_custom_call" | custom-call | tf_op jit(solution)/shard_map/pallas_call | solution.py:450

commit v3 on v2

--- a/solution.py
+++ b/solution.py
@@ -20,6 +20,7 @@
 WIDTH = HEADS_DEV * HEAD_DIM
 NZ, NX, NY, PLANE = 16, 4, 4, 8
 CHUNKS = 7
+FAR_FIRST = (4, 5, 2, 3, 6, 7, 1, 0)
 PER = SLOTS // CHUNKS
 
 MESH = pl.DeviceIdType.MESH
@@ -101,9 +102,10 @@
 
 
 def step_kernel(names, *refs):
-    (store, kw, vw, owner_s, row_s, valid_s, queries_h, grads_h, attended_h, sums_out) = refs[:10]
+    (store_h, kw, vw, owner_s, row_s, valid_s, queries_h, grads_h, attended_h, sums_h) = refs[:10]
     planes, named = refs[10:25], dict(zip(names, refs[25:]))
-    S = lambda name: named[name]
+    S = named.__getitem__
+    store = S("store")
     tab_v, tab_s, stage, got, wall = map(S, ("tab_v", "tab_s", "stage", "got", "wall"))
     nb, weights, queries, grads, attended = map(S, ("nb", "weights", "queries", "grads", "attended"))
     ups = [store] + [planes[2 * s - 2] for s in range(1, 8)] + [planes[14]]
@@ -121,13 +123,16 @@
     z_peer = [(((z + t) % NZ) * PLANE + r, y) for t in range(1, NZ)]
 
     local_sem = S("local_sem")
+    load_store = pltpu.make_async_copy(store_h, store, local_sem.at[3])
+    load_store.start()
     loads = [
         pltpu.make_async_copy(queries_h, queries, local_sem.at[0]),
         pltpu.make_async_copy(grads_h, grads, local_sem.at[1]),
     ]
     for copy in loads:
         copy.start()
-    greet(peer[1:] + z_peer + [yup, ydn])
+    greet([zup, zdn, yup, ydn] + peer[1:])
+    load_store.wait()
 
     lane = lax.broadcasted_iota(jnp.int32, (1, 128), 1)
     wanted = jnp.zeros((1, 128), jnp.int32)
@@ -225,22 +230,26 @@
             local = pltpu.make_async_copy(tab_v, tab_s, local_sem.at[2])
             local.start()
             local.wait()
-        for way in range(1 if s in (0, 8) else 2):
-            buf = (ups, dns)[way][s]
-            far = (z + NZ - s) % NZ if way == 0 else (z + s) % NZ
-            for t in range(PLANE):
+        for t in FAR_FIRST:
+            for way in range(1 if s in (0, 8) else 2):
+                buf = (ups, dns)[way][s]
+                far = (z + NZ - s) % NZ if way == 0 else (z + s) % NZ
                 entry = buf[tab_s[(r + t) % PLANE, 0, far * PLANE + r]]
                 if t == 0:
                     got[r, place(s, way)] = entry
                 else:
                     stage[t, place(s, way)] = entry
-        for t in range(1, PLANE):
-            for copy in (weight_plane(s, t), cell_plane(s, t)):
+            if t > 0:
+                copy = cell_plane(s, t)
                 copy.start()
                 sent.append(copy)
-        if s >= 2:
-            place_weights(s - 2)
-    place_weights(7)
+        for late in () if s == 0 else (s - 1,) if s < 8 else (7, 8):
+            for t in range(1, PLANE):
+                copy = weight_plane(late, t)
+                copy.start()
+                sent.append(copy)
+        if s >= 3:
+            place_weights(s - 3)
     for s in range(9):
         for t in range(1, PLANE):
             cell_plane(s, t).wait_recv()
@@ -264,10 +273,11 @@
             copy.start()
             sent.append(copy)
 
-    ahead = 3
+    ahead, behind = 4, 2
     for g in range(ahead):
         send_own(g)
-    place_weights(8)
+    for s in (6, 7, 8):
+        place_weights(s)
     for copy in loads:
         copy.wait()
     stores = []
@@ -292,10 +302,15 @@
         sent.append(copy)
         if g + ahead < CHUNKS:
             send_own(g + ahead)
-        if g > 0:
-            attend(g - 1)
-    attend(CHUNKS - 1)
-
+        if g >= behind:
+            attend(g - behind)
+    for g in range(CHUNKS - behind, CHUNKS):
+        attend(g)
+
+    for copy in sent:
+        copy.wait_send()
+    for copy in stores:
+        copy.wait()
     rows_t, cot, total = S("rows_t"), S("cot"), S("total")
     c_send, c_recv, x_send, x_recv = map(S, ("c_send", "c_recv", "x_send", "x_recv"))
     own, z_send, z_recv = map(S, ("own", "z_send", "z_recv"))
@@ -350,14 +365,16 @@
         fin[:, h * 256 + 128 : h * 256 + 256] = done[8:]
     last = remote(fin, fin_in, S("fs"), S("fr"), mate)
     last.start()
-    for copy in sent + core_copies + x_copies + z_copies:
+    for copy in core_copies + x_copies + z_copies:
         copy.wait_send()
-    for copy in stores:
-        copy.wait()
     last.wait()
     even = c == 0
-    sums_out[0] = jnp.where(even, fin[...], fin_in[...])
-    sums_out[1] = jnp.where(even, fin_in[...], fin[...])
+    sums = S("sums")
+    sums[0] = jnp.where(even, fin[...], fin_in[...])
+    sums[1] = jnp.where(even, fin_in[...], fin[...])
+    copy = pltpu.make_async_copy(sums, sums_h, local_sem.at[4])
+    copy.start()
+    copy.wait()
 
 
 def step(queries, out_grad, store, key_weight, value_weight, owner, row, valid):
@@ -385,7 +402,9 @@
         "z_recv": VM((2, NZ - 1, 16, 128), BF16),
         "fin": VM((8, WIDTH), F32),
         "fin_in": VM((8, WIDTH), F32),
-        "local_sem": dma((3,)),
+        "local_sem": dma((5,)),
+        "store": VM((16, NB_LEN, 128), BF16),
+        "sums": VM((2, 8, WIDTH), F32),
         "out_sem": dma((CHUNKS,)),
         "fs": dma,
         "fr": dma,
@@ -411,8 +430,8 @@
             jax.ShapeDtypeStruct((BLOCKS * BLOCK_LEN, WIDTH), BF16),
             jax.ShapeDtypeStruct((2, 8, WIDTH), F32),
         ),
-        in_specs=[VSPEC] * 3 + [SSPEC] * 3 + [anywhere] * 2,
-        out_specs=(anywhere, VSPEC),
+        in_specs=[anywhere] + [VSPEC] * 2 + [SSPEC] * 3 + [anywhere] * 2,
+        out_specs=(anywhere, anywhere),
         scratch_shapes=[VM((16, NB_LEN, 128), BF16)] * 15 + list(scratch.values()),
         compiler_params=pltpu.CompilerParams(
             collective_id=0, has_side_effects=True, vmem_limit_bytes=VLIMIT
@@ -420,10 +439,12 @@
     )(store, key_weight, value_weight, owner.T, row.T, valid.T, queries, out_grad)
 
 
-def finish_kernel(attended_in, sums, attended, key_out, value_out, held, sem_in, sem_out):
+def finish_kernel(attended_in, sums_in, attended, key_out, value_out, held, sums, key, value, sem_in, sem_out, sem):
     count = sem_in.shape[0]
     size = held.shape[0] // count
     pieces = [pl.ds(i * size, size) for i in range(count)]
+    first = pltpu.make_async_copy(sums_in, sums, sem.at[0])
+    first.start()
     inward = [
         pltpu.make_async_copy(attended_in.at[piece], held.at[piece], sem_in.at[i])
         for i, piece in enumerate(pieces)
@@ -432,11 +453,18 @@
         pltpu.make_async_copy(held.at[piece], attended.at[piece], sem_out.at[i])
         for i, piece in enumerate(pieces)
     ]
+    outward += [
+        pltpu.make_async_copy(key, key_out, sem.at[1]),
+        pltpu.make_async_copy(value, value_out, sem.at[2]),
+    ]
     for copy in inward:
         copy.start()
     low = lax.axis_index("dp") % 2 == 0
-    key_out[...] = jnp.where(low, sums[0, :4], sums[0, 4:])
-    value_out[...] = jnp.where(low, sums[1, :4], sums[1, 4:])
+    first.wait()
+    key[...] = jnp.where(low, sums[0, :4], sums[0, 4:])
+    value[...] = jnp.where(low, sums[1, :4], sums[1, 4:])
+    for copy in outward[count:]:
+        copy.start()
     for i in range(count):
         inward[i].wait()
         outward[i].start()
@@ -447,16 +475,25 @@
 def finish(attended, sums):
     anywhere = pl.BlockSpec(memory_space=pl.ANY)
     dma = pltpu.SemaphoreType.DMA
+    gradient = (4, WIDTH)
     return pl.pallas_call(
         finish_kernel,
         out_shape=(
             jax.ShapeDtypeStruct(attended.shape, BF16),
-            jax.ShapeDtypeStruct((4, WIDTH), F32),
-            jax.ShapeDtypeStruct((4, WIDTH), F32),
+            jax.ShapeDtypeStruct(gradient, F32),
+            jax.ShapeDtypeStruct(gradient, F32),
         ),
-        in_specs=[anywhere, VSPEC],
-        out_specs=(anywhere, VSPEC, VSPEC),
-        scratch_shapes=[VM(attended.shape, BF16), dma((CHUNKS,)), dma((CHUNKS,))],
+        in_specs=[anywhere] * 2,
+        out_specs=(anywhere,) * 3,
+        scratch_shapes=[
+            VM(attended.shape, BF16),
+            VM(sums.shape, F32),
+            VM(gradient, F32),
+            VM(gradient, F32),
+            dma((CHUNKS,)),
+            dma((CHUNKS,)),
+            dma((3,)),
+        ],
         compiler_params=pltpu.CompilerParams(vmem_limit_bytes=VLIMIT),
     )(attended, sums)
 

time: 126 us -> 120 us (0.952)
  Pallas kernels: 125 us -> 119 us
    pallas_call x1, Pallas kernels: 122 us -> 117 us  [step(): pl.pallas_call(functools.partial(step_kernel, tuple(scratch)), out_shape=...]
where the time goes in v3:
time: 120 us
  Pallas kernels  119 us (99%)
    pallas_call x1, Pallas kernels, step(): pl.pallas_call(functools.partial(step_kernel, tuple(scratch)), out_shape=...  117 us

profile of v3, /device:TPU:1, one launch (start us, length us, event | category | flops | bytes accessed | tf_op | source)
XLA Modules:
  0.0 120.2 jit_solution(6951596416482988994)
XLA Ops:
  0.6 117.2 %shard_map.103 = (bf16[896,512]{1,0:T(8,128)(2,1)}, f32[2,8,512]{2,1,0:T(8,128)}) custom-call(bf16[16,64,128]{2,1,0:T(8,128)(2,1)} %refs_0_.1, bf16[4,512]{1,0:T(4,128)(2,1)} %refs_1_.1, bf16[4,512]{1,0:T(4,128)(2,1)} %refs_2_.1, s32[2,14]{1,0:T(2,128)} %bitcast.3, s32[2,14]{1,0:T(2,128)} %bitcast.4, s32[2,14]{1,0:T(2,128)} %bitcast.5, ...), custom_call_target="tpu_custom_call" | custom-call | tf_op jit(solution)/shard_map/pallas_call | solution.py:427
  117.9 2.2 %shard_map.104 = (bf16[896,512]{1,0:T(8,128)(2,1)}, f32[4,512]{1,0:T(4,128)}, f32[4,512]{1,0:T(4,128)}) custom-call(bf16[896,512]{1,0:T(8,128)(2,1)} %get-tuple-element.5.attended_in, f32[2,8,512]{2,1,0:T(8,128)} %get-tuple-element.6.sums_in), custom_call_target="tpu_custom_call" | custom-call | tf_op jit(solution)/shard_map/pallas_call | solution.py:479

commit v4 on v3

--- a/solution.py
+++ b/solution.py
@@ -27,8 +27,6 @@
 F32 = jnp.float32
 BF16 = jnp.bfloat16
 VM = pltpu.VMEM
-VSPEC = pl.BlockSpec(memory_space=pltpu.VMEM)
-SSPEC = pl.BlockSpec(memory_space=pltpu.SMEM)
 VLIMIT = 56 * 2**20
 
 
@@ -41,13 +39,6 @@
         device_id=device,
         device_id_type=MESH,
     )
-
-
-def greet(devices):
-    barrier = pltpu.get_barrier_semaphore()
-    for device in devices:
-        pl.semaphore_signal(barrier, inc=1, device_id=device, device_id_type=MESH)
-    pl.semaphore_wait(barrier, len(devices))
 
 
 def dot(a, b):
@@ -102,14 +93,15 @@
 
 
 def step_kernel(names, *refs):
-    (store_h, kw, vw, owner_s, row_s, valid_s, queries_h, grads_h, attended_h, sums_h) = refs[:10]
-    planes, named = refs[10:25], dict(zip(names, refs[25:]))
+    (store_h, kw_h, vw_h, owner_h, row_h, valid_h, queries_h, grads_h, attended_h, sums_h) = refs[:10]
+    planes, named = refs[10:24], dict(zip(names, refs[24:]))
     S = named.__getitem__
-    store = S("store")
+    store, kw, vw = map(S, ("store", "kw", "vw"))
+    owner_s, row_s, valid_s = map(S, ("owner_s", "row_s", "valid_s"))
     tab_v, tab_s, stage, got, wall = map(S, ("tab_v", "tab_s", "stage", "got", "wall"))
     nb, weights, queries, grads, attended = map(S, ("nb", "weights", "queries", "grads", "attended"))
-    ups = [store] + [planes[2 * s - 2] for s in range(1, 8)] + [planes[14]]
-    dns = [store] + [planes[2 * s - 1] for s in range(1, 8)] + [planes[14]]
+    ups = [store] + [planes[2 * s - 2] for s in range(1, 8)]
+    dns = [store] + [planes[2 * s - 1] for s in range(1, 8)]
     me = lax.axis_index("dp")
     y = lax.axis_index("mp")
     z, r = me // PLANE, me % PLANE
@@ -123,16 +115,34 @@
     z_peer = [(((z + t) % NZ) * PLANE + r, y) for t in range(1, NZ)]
 
     local_sem = S("local_sem")
-    load_store = pltpu.make_async_copy(store_h, store, local_sem.at[3])
-    load_store.start()
+    friends = [zup, zdn, yup, ydn] + peer[1:]
+    barrier = pltpu.get_barrier_semaphore()
+    for friend in friends:
+        pl.semaphore_signal(barrier, inc=1, device_id=friend, device_id_type=MESH)
+    early = [
+        pltpu.make_async_copy(here, there, S("early_sem").at[i])
+        for i, (here, there) in enumerate(
+            (
+                (store_h, store),
+                (kw_h, kw),
+                (vw_h, vw),
+                (owner_h, owner_s),
+                (row_h, row_s),
+                (valid_h, valid_s),
+            )
+        )
+    ]
+    for copy in early:
+        copy.start()
     loads = [
         pltpu.make_async_copy(queries_h, queries, local_sem.at[0]),
         pltpu.make_async_copy(grads_h, grads, local_sem.at[1]),
     ]
     for copy in loads:
         copy.start()
-    greet([zup, zdn, yup, ydn] + peer[1:])
-    load_store.wait()
+    pl.semaphore_wait(barrier, len(friends))
+    for copy in early:
+        copy.wait()
 
     lane = lax.broadcasted_iota(jnp.int32, (1, 128), 1)
     wanted = jnp.zeros((1, 128), jnp.int32)
@@ -149,6 +159,18 @@
     ]
     for copy in tab_copies:
         copy.start()
+
+    far_out, far_in = S("far_out"), S("far_in")
+    tab_near = [
+        remote(tab_v, S("near_v").at[way], S("near_ss").at[way], S("near_rs").at[way], (zup, zdn)[way])
+        for way in range(2)
+    ]
+
+    def far_cells(way):
+        half = pl.ds(way * 4, 4)
+        return remote(
+            far_out.at[half], far_in.at[half], S("far_s").at[way], S("far_r").at[way], (zup, zdn)[way]
+        )
 
     def ring(s, way, part):
         bufs = (ups, dns)[way]
@@ -182,7 +204,7 @@
 
     def cell_plane(s, t):
         return remote(
-            stage.at[t, cut_of(s)],
+            far_in.at[pl.ds((r + t) % PLANE, 1)] if s == 8 else stage.at[t, cut_of(s)],
             got.at[r, cut_of(s)],
             S("cell_s").at[t, s],
             S("cell_r").at[t, s],
@@ -218,9 +240,9 @@
                 sent.append(copy)
         for part in range(2):
             for way in range(2):
-                if s > 0 and not (s == 8 and part != way):
+                if 0 < s < 8:
                     ring(s - 1, way, part).wait_recv()
-                if s < 8 and not (s == 7 and part != way):
+                if s < 7:
                     copy = ring(s, way, part)
                     copy.start()
                     sent.append(copy)
@@ -230,8 +252,30 @@
             local = pltpu.make_async_copy(tab_v, tab_s, local_sem.at[2])
             local.start()
             local.wait()
+            for copy in tab_near:
+                copy.start()
+                sent.append(copy)
+        if s == 1:
+            for copy in tab_near:
+                copy.wait_recv()
+            local = pltpu.make_async_copy(S("near_v"), S("near_s"), local_sem.at[3])
+            local.start()
+            local.wait()
+        if s == 7:
+            for way in range(2):
+                buf = (ups, dns)[way][7]
+                far = (z + NZ - 7) % NZ if way == 0 else (z + 7) % NZ
+                for i in range(way * 4, way * 4 + 4):
+                    far_out[i] = buf[S("near_s")[1 - way, i, 0, far * PLANE + r]]
+                copy = far_cells(way)
+                copy.start()
+                sent.append(copy)
+        if s == 8:
+            for way in range(2):
+                far_cells(way).wait_recv()
+            got[r, 15] = far_in[r]
         for t in FAR_FIRST:
-            for way in range(1 if s in (0, 8) else 2):
+            for way in range((2, 1)[s == 0] if s < 8 else 0):
                 buf = (ups, dns)[way][s]
                 far = (z + NZ - s) % NZ if way == 0 else (z + s) % NZ
                 entry = buf[tab_s[(r + t) % PLANE, 0, far * PLANE + r]]
@@ -258,10 +302,11 @@
         part = nb.at[y, pl.ds(g * PER, PER)]
         return remote(part, part, S("ys_s").at[way, g], S("ys_r").at[way, g], (yup, ydn)[way])
 
-    def forward_y(g):
-        origin = (y + NY - 1) % NY if g % 2 == 0 else (y + 1) % NY
-        part = nb.at[origin, pl.ds(g * PER, PER)]
-        return remote(part, part, S("yf_s").at[g], S("yf_r").at[g], (yup, ydn)[g % 2])
+    def forward_y(g, way):
+        origin = (y + NY - 1) % NY if way == 0 else (y + 1) % NY
+        half = PER // 2
+        part = nb.at[origin, pl.ds(g * PER + way * half, half)]
+        return remote(part, part, S("yf_s").at[way, g], S("yf_r").at[way, g], (yup, ydn)[way])
 
     def send_own(g):
         for i in range(g * PER, (g + 1) * PER):
@@ -273,7 +318,7 @@
             copy.start()
             sent.append(copy)
 
-    ahead, behind = 4, 2
+    ahead, behind = 3, 2
     for g in range(ahead):
         send_own(g)
     for s in (6, 7, 8):
@@ -283,7 +328,8 @@
     stores = []
 
     def attend(g):
-        forward_y(g).wait_recv()
+        for way in range(2):
+            forward_y(g, way).wait_recv()
         attend_chunk(
             g, nb, weights, queries, grads, valid_s, attended, S("cot"), S("rows_t")
         )
@@ -297,9 +343,9 @@
     for g in range(CHUNKS):
         for way in range(2):
             own_y(g, way).wait_recv()
-        copy = forward_y(g)
-        copy.start()
-        sent.append(copy)
+            copy = forward_y(g, way)
+            copy.start()
+            sent.append(copy)
         if g + ahead < CHUNKS:
             send_own(g + ahead)
         if g >= behind:
@@ -403,6 +449,16 @@
         "fin": VM((8, WIDTH), F32),
         "fin_in": VM((8, WIDTH), F32),
         "local_sem": dma((5,)),
+        "near_v": VM((2, PLANE, 1, 128), jnp.int32),
+        "near_s": pltpu.SMEM((2, PLANE, 1, 128), jnp.int32),
+        "far_out": VM((PLANE, NB_LEN, 128), BF16),
+        "far_in": VM((PLANE, NB_LEN, 128), BF16),
+        "early_sem": dma((6,)),
+        "kw": VM((4, WIDTH), BF16),
+        "vw": VM((4, WIDTH), BF16),
+        "owner_s": pltpu.SMEM((NEIGH, BLOCKS), jnp.int32),
+        "row_s": pltpu.SMEM((NEIGH, BLOCKS), jnp.int32),
+        "valid_s": pltpu.SMEM((NEIGH, BLOCKS), jnp.int32),
         "store": VM((16, NB_LEN, 128), BF16),
         "sums": VM((2, 8, WIDTH), F32),
         "out_sem": dma((CHUNKS,)),
@@ -410,13 +466,15 @@
         "fr": dma,
     }
     for send, recv, shape in (
-        ("ring_s", "ring_r", (2, 8, 2)),
+        ("ring_s", "ring_r", (2, 7, 2)),
+        ("near_ss", "near_rs", (2,)),
+        ("far_s", "far_r", (2,)),
         ("wring_s", "wring_r", (2, 8)),
         ("cell_s", "cell_r", (PLANE, 9)),
         ("wc_s", "wc_r", (PLANE, 9)),
         ("tab_ss", "tab_rs", (PLANE,)),
         ("ys_s", "ys_r", (2, CHUNKS)),
-        ("yf_s", "yf_r", (CHUNKS,)),
+        ("yf_s", "yf_r", (2, CHUNKS)),
         ("cs", "cr", (2,)),
         ("xs", "xr", (2, NX - 1)),
         ("zs", "zr", (2, NZ - 1)),
@@ -430,9 +488,9 @@
             jax.ShapeDtypeStruct((BLOCKS * BLOCK_LEN, WIDTH), BF16),
             jax.ShapeDtypeStruct((2, 8, WIDTH), F32),
         ),
-        in_specs=[anywhere] + [VSPEC] * 2 + [SSPEC] * 3 + [anywhere] * 2,
+        in_specs=[anywhere] * 8,
         out_specs=(anywhere, anywhere),
-        scratch_shapes=[VM((16, NB_LEN, 128), BF16)] * 15 + list(scratch.values()),
+        scratch_shapes=[VM((16, NB_LEN, 128), BF16)] * 14 + list(scratch.values()),
         compiler_params=pltpu.CompilerParams(
             collective_id=0, has_side_effects=True, vmem_limit_bytes=VLIMIT
         ),

time: 120 us -> 119 us (level)
    pallas_call x1, Pallas kernels: 117 us -> 115 us  [step(): pl.pallas_call(functools.partial(step_kernel, tuple(scratch)), out_shape=...]
where the time goes in v4:
time: 119 us; the launch traced here: 118 us
  Pallas kernels  118 us (99%)
    pallas_call x1, Pallas kernels, step(): pl.pallas_call(functools.partial(step_kernel, tuple(scratch)), out_shape=...  115 us

profile of v4, /device:TPU:1, one launch (start us, length us, event | category | flops | bytes accessed | tf_op | source)
XLA Modules:
  0.0 118.5 jit_solution(8806094372987243347)
XLA Ops:
  0.6 115.5 %shard_map.103 = (bf16[896,512]{1,0:T(8,128)(2,1)}, f32[2,8,512]{2,1,0:T(8,128)}) custom-call(bf16[16,64,128]{2,1,0:T(8,128)(2,1)} %refs_0_.1, bf16[4,512]{1,0:T(4,128)(2,1)} %refs_1_.1, bf16[4,512]{1,0:T(4,128)(2,1)} %refs_2_.1, s32[2,14]{1,0:T(2,128)} %bitcast.3, s32[2,14]{1,0:T(2,128)} %bitcast.4, s32[2,14]{1,0:T(2,128)} %bitcast.5, ...), custom_call_target="tpu_custom_call" | custom-call | tf_op jit(solution)/shard_map/pallas_call | solution.py:485
  116.1 2.2 %shard_map.104 = (bf16[896,512]{1,0:T(8,128)(2,1)}, f32[4,512]{1,0:T(4,128)}, f32[4,512]{1,0:T(4,128)}) custom-call(bf16[896,512]{1,0:T(8,128)(2,1)} %get-tuple-element.5.attended_in, f32[2,8,512]{2,1,0:T(8,128)} %get-tuple-element.6.sums_in), custom_call_target="tpu_custom_call" | custom-call | tf_op jit(solution)/shard_map/pallas_call | solution.py:537

commit v5 on v4

--- a/solution.py
+++ b/solution.py
@@ -287,7 +287,7 @@
                 copy = cell_plane(s, t)
                 copy.start()
                 sent.append(copy)
-        for late in () if s == 0 else (s - 1,) if s < 8 else (7, 8):
+        for late in () if s in (0, 7) else (s - 1,) if s < 8 else (6, 7, 8):
             for t in range(1, PLANE):
                 copy = weight_plane(late, t)
                 copy.start()
@@ -321,10 +321,6 @@
     ahead, behind = 3, 2
     for g in range(ahead):
         send_own(g)
-    for s in (6, 7, 8):
-        place_weights(s)
-    for copy in loads:
-        copy.wait()
     stores = []
 
     def attend(g):
@@ -348,6 +344,11 @@
             sent.append(copy)
         if g + ahead < CHUNKS:
             send_own(g + ahead)
+        if g == behind:
+            for s in (6, 7, 8):
+                place_weights(s)
+            for copy in loads:
+                copy.wait()
         if g >= behind:
             attend(g - behind)
     for g in range(CHUNKS - behind, CHUNKS):

time: 119 us -> 119 us (level)
  no operation moved by 1% of the time
where the time goes in v5:
time: 119 us
  Pallas kernels  118 us (99%)
    pallas_call x1, Pallas kernels, step(): pl.pallas_call(functools.partial(step_kernel, tuple(scratch)), out_shape=...  116 us

profile of v5, /device:TPU:1, one launch (start us, length us, event | category | flops | bytes accessed | tf_op | source)
XLA Modules:
  0.0 118.6 jit_solution(2909965453772795099)
XLA Ops:
  0.6 115.7 %shard_map.103 = (bf16[896,512]{1,0:T(8,128)(2,1)}, f32[2,8,512]{2,1,0:T(8,128)}) custom-call(bf16[16,64,128]{2,1,0:T(8,128)(2,1)} %refs_0_.1, bf16[4,512]{1,0:T(4,128)(2,1)} %refs_1_.1, bf16[4,512]{1,0:T(4,128)(2,1)} %refs_2_.1, s32[2,14]{1,0:T(2,128)} %bitcast.3, s32[2,14]{1,0:T(2,128)} %bitcast.4, s32[2,14]{1,0:T(2,128)} %bitcast.5, ...), custom_call_target="tpu_custom_call" | custom-call | tf_op jit(solution)/shard_map/pallas_call | solution.py:486
  116.3 2.2 %shard_map.104 = (bf16[896,512]{1,0:T(8,128)(2,1)}, f32[4,512]{1,0:T(4,128)}, f32[4,512]{1,0:T(4,128)}) custom-call(bf16[896,512]{1,0:T(8,128)(2,1)} %get-tuple-element.5.attended_in, f32[2,8,512]{2,1,0:T(8,128)} %get-tuple-element.6.sums_in), custom_call_target="tpu_custom_call" | custom-call | tf_op jit(solution)/shard_map/pallas_call | solution.py:538
